TPU v7x, 32 devices: a whole 2x2x4 slice. The times are simulated.
32 devices in a mesh: groups: 2 (over y), tm: 8 (over z, x), cells: 2 (over core).
Axes of the slice: x: 2, y: 2, z: 4, core: 2. Of those that a mesh axis runs over, the one named last changes fastest.
Arguments:
- propagator: bfloat16 [272, 48, 4, 256], P(('groups', 'tm'), None, None, 'cells'), parts along dimension 0, as said below
- tile_blocks: int32 [272, 2], P(('groups', 'tm')), parts along dimension 0, may hold values from 0 to 15, as said below
- histories: bfloat16 [16, 12, 48], P('tm'), may hold values from -6 to 6
Outputs:
- concentration: float32 [32, 12, 4, 256], P(('groups', 'tm'), None, None, 'cells'), parts along dimension 0
There are 2 independent parts, one for each index of `groups`. A program takes and returns all parts, laid end to end along the dimension named above; an argument that names none is the same for every part. Nothing has to cross between parts.
Inputs may be any that keep to these rules, and one draw needn't show every extreme that they name: `tile_blocks`: rows s * 17 to (s + 1) * 17 - 1 belong to two mirrored source blocks p and 15 - p, where p runs over a permutation of 0 to 7 from one such row group to the next; for each of the two source blocks every arrival block from it up to 15 appears in exactly one row, rows in any order. Tile n holds the propagator from source block tile_blocks[n, 0] to arrival block tile_blocks[n, 1].
All inputs are finite; a program needn't handle non-finite values.
Results may differ from a plain program's by a relative error of at most 0.0003.
Values may be sent and summed in bfloat16 or wider, within the bound.
A program may use at most 64 MiB of HBM per device.

v0:
```python
import jax
import jax.numpy as jnp
from jax import lax
from jax.sharding import PartitionSpec as P


def shards(propagator, tile_blocks, histories):
    all_histories = lax.all_gather(histories, "tm", axis=0, tiled=True)
    block_count = all_histories.shape[0]
    tracer_count = all_histories.shape[1]
    slot_count, source_width, months, cell_count = propagator.shape
    tile_rows = propagator.reshape(slot_count, source_width, months * cell_count)
    sources = tile_blocks[:, 0]
    arrivals = tile_blocks[:, 1]
    selector = (sources[:, None] == jnp.arange(block_count, dtype=jnp.int32)[None, :]).astype(
        jnp.bfloat16
    )
    chosen = jnp.dot(
        selector,
        all_histories.reshape(block_count, tracer_count * source_width),
        preferred_element_type=jnp.float32,
    )
    chosen = chosen.astype(jnp.bfloat16).reshape(slot_count, tracer_count, source_width)
    contribution = jnp.einsum("nrk,nkm->nrm", chosen, tile_rows, preferred_element_type=jnp.float32)
    partial_sums = (
        jnp.zeros((block_count, tracer_count, months * cell_count), jnp.float32)
        .at[arrivals]
        .add(contribution)
    )
    owned = lax.psum_scatter(partial_sums, "tm", scatter_dimension=0, tiled=True)
    return owned.reshape(owned.shape[0], tracer_count, months, cell_count)


def solution(mesh):
    in_specs = (
        P(("groups", "tm"), None, None, "cells"),
        P(("groups", "tm"), None),
        P("tm", None, None),
    )
    out_specs = P(("groups", "tm"), None, None, "cells")
    return jax.shard_map(shards, mesh=mesh, in_specs=in_specs, out_specs=out_specs, check_vma=False)
```

profile of v0, /device:TPU:0, one launch (start us, length us, event | category | flops | bytes accessed | tf_op | source)
XLA Modules:
  0.0 117.3 jit_solution(11963903710635323625)
XLA Ops:
  6.5 0.0 reduce-scatter.2.cloned.1.call-start
  6.5 0.8 slice_bitcast_fusion
  7.3 0.7 copy.9
  8.0 32.3 %all_gather.3 = bf16[16,12,48]{2,1,0:T(8,128)(2,1)S(1)} all-gather(bf16[2,12,48]{2,1,0:T(8,128)(2,1)S(1)} %copy.9), channel_id=1, replica_groups=mesh['groups'=2,'tm'=8,'cells'=2] {'tm'}, dimensions={0}, use_global_device_ids=true | all-gather | bytes 20736 | tf_op jit(solution)/shard_map/all_gather | solution.py:8
  40.3 0.1 reshape.12
  40.4 0.2 convolution_convert_fusion
  40.6 0.1 reshape.13
  40.7 1.7 %reshape.14 = bf16[17,48,512]{2,1,0:T(8,128)(2,1)S(1)} reshape(bf16[17,48,4,128]{3,2,1,0:T(4,128)(2,1)} %param.3) | data formatting | bytes 1671168 | tf_op jit(solution)/shard_map/reshape | solution.py:12
  42.4 0.2 fusion.2
  42.6 0.1 broadcast_in_dim.2
  42.7 2.1 %scatter_fusion = f32[16,12,512]{2,1,0:T(8,128)S(1)} fusion(f32[16,12,512]{2,1,0:T(8,128)S(1)} %broadcast_in_dim.2, s32[17]{0:T(128)S(1)} %get-tuple-element.6, f32[17,12,512]{2,1,0:T(8,128)S(1)} %fusion.2), kind=kCustom, calls=%fused_computation | custom fusion | flops 104448 | bytes 1253444 | tf_op jit(solution)/shard_map/scatter-add | solution.py:28
  44.8 0.0 copy-start
  44.8 0.8 copy-done
  45.6 0.0 reduce-scatter.2.cloned.1.call-update
  45.6 63.4 %reduce-scatter.2.cloned.1.call-done = f32[2,12,512]{2,1,0:T(8,128)} async-done(((f32[16,12,512]{2,1,0:T(8,128)}), f32[2,12,512]{2,1,0:T(8,128)}) %reduce-scatter.2.cloned.1.call-update) | async-done | bytes 49168 | tf_op jit(solution)/shard_map/reduce_scatter | solution.py:30
  109.0 1.5 %reshape.24 = f32[2,12,4,128]{3,2,1,0:T(4,128)} reshape(f32[2,12,512]{2,1,0:T(8,128)} %reduce-scatter.2.cloned.1.call-done) | data formatting | bytes 98304 | tf_op jit(solution)/shard_map/reshape | solution.py:31
Async XLA Ops:
  6.5 102.5 %reduce-scatter.2.cloned.1.call-start = ((), (), s32[]{:S(2)}) async-start(), calls=%async_computation.1 | async-start | bytes 589824 | tf_op jit(solution)/shard_map/reduce_scatter | solution.py:30
  44.8 0.8 copy-start
Sparse Core Ops, SparseCore 0:
  45.8 63.2 reduce-scatter.1
where the time goes:
time: 118 us; the launch traced here: 117 us
  waiting for transfers between devices  63.4 us (54%)
  blocking collectives  32.3 us (27%)
  between operations  13.4 us (11%)
  local copies, waits for them, and re-layouts  4.92 us (4%)
  other arithmetic  2.87 us (2%)
    reduce_scatter x1, waiting for transfers between devices, shards(): lax.psum_scatter(partial_sums, 'tm', scatter_dimension=0, tiled=True)  63.4 us
    all_gather x1, blocking collectives, shards(): all_histories = lax.all_gather(histories, 'tm', axis=0, tiled=True)  32.3 us
  transfers between devices with their start and end apart: 1, of which 1 were waited for; matrix products, arithmetic and copies ran while one was open for 0% of the time, Pallas kernels for 0%

commit v1 on v0

--- a/solution.py
+++ b/solution.py
@@ -5,7 +5,16 @@
 
 
 def shards(propagator, tile_blocks, histories):
-    all_histories = lax.all_gather(histories, "tm", axis=0, tiled=True)
+    ways = lax.axis_size("tm")
+    up = [(d, (d + 1) % ways) for d in range(ways)]
+    down = [(d, (d - 1) % ways) for d in range(ways)]
+    earlier, later = ([histories], [histories])
+    for _ in range(ways // 2):
+        earlier.append(lax.ppermute(earlier[-1], "tm", up))
+    for _ in range((ways - 1) // 2):
+        later.append(lax.ppermute(later[-1], "tm", down))
+    line = jnp.concatenate([*earlier[::-1], *later[1:]], axis=0)
+    all_histories = jnp.roll(line, (lax.axis_index("tm") - ways // 2) * histories.shape[0], axis=0)
     block_count = all_histories.shape[0]
     tracer_count = all_histories.shape[1]
     slot_count, source_width, months, cell_count = propagator.shape

time: 118 us -> 106 us (0.90)
  blocking collectives: 32.3 us -> 0 us
  starting transfers between devices: 0.01 us -> 15.4 us
  waiting for transfers between devices: 63.4 us -> 68.8 us
    all_gather x1 -> x0, blocking collectives: 32.3 us -> none  [shards(): all_histories = lax.all_gather(histories, 'tm', axis=0, tiled=True)]
    ppermute x0 -> x7, starting transfers between devices: none -> 15.4 us  [the longest x3 12.5 us: shards(): later.append(lax.ppermute(later[-1], 'tm', down))]
    ppermute x0 -> x7, waiting for transfers between devices: none -> 8.86 us  [the longest x4 8.85 us: shards(): earlier.append(lax.ppermute(earlier[-1], 'tm', up))]
    reduce_scatter x1, waiting for transfers between devices: 63.4 us -> 59.9 us  [shards(): lax.psum_scatter(partial_sums, 'tm', scatter_dimension=0, tiled=True)]
  transfers between devices with their start and end apart: 1 -> 8, of which waited for: 1 -> 5; matrix products, arithmetic and copies ran while one was open for 0% -> 2% of each run, Pallas kernels for 0% -> 0%
where the time goes in v1:
time: 106 us; the launch traced here: 105 us
  waiting for transfers between devices  68.8 us (65%)
  starting transfers between devices  15.4 us (15%)
  between operations  13.5 us (13%)
  local copies, waits for them, and re-layouts  4.5 us (4%)
  other arithmetic  2.87 us (3%)
    reduce_scatter x1, waiting for transfers between devices, shards(): lax.psum_scatter(partial_sums, 'tm', scatter_dimension=0, tiled=True)  59.9 us
    ppermute x3, starting transfers between devices, shards(): later.append(lax.ppermute(later[-1], 'tm', down))  12.5 us
    ppermute x4, waiting for transfers between devices, shards(): earlier.append(lax.ppermute(earlier[-1], 'tm', up))  8.85 us
    ppermute x4, starting transfers between devices, shards(): earlier.append(lax.ppermute(earlier[-1], 'tm', up))  2.95 us
  transfers between devices with their start and end apart: 8, of which 5 were waited for; matrix products, arithmetic and copies ran while one was open for 2% of the time, Pallas kernels for 0%

profile of v1, /device:TPU:0, one launch (start us, length us, event | category | flops | bytes accessed | tf_op | source)
XLA Modules:
  0.0 105.5 jit_solution(1086709632402741849)
XLA Ops:
  6.5 2.9 %collective-permute-start = (bf16[2,12,48]{2,0,1:T(2,128)(2,1)}, bf16[2,12,48]{2,0,1:T(2,128)(2,1)S(1)}, u32[]{:S(2)}, u32[]{:S(2)}) collective-permute-start(bf16[2,12,48]{2,0,1:T(2,128)(2,1)} %param.5), channel_id=1, source_target_pairs={{0,2},{2,4},{4,6},{6,8},{8,10},{10,12},{12,14},{14,0},{1,3},{3,5},... | collective-permute-start | bytes 6920 | tf_op jit(solution)/shard_map/ppermute | solution.py:13
  9.5 3.0 %collective-permute-start.4 = (bf16[2,12,48]{2,0,1:T(2,128)(2,1)}, bf16[2,12,48]{2,0,1:T(2,128)(2,1)S(1)}, u32[]{:S(2)}, u32[]{:S(2)}) collective-permute-start(bf16[2,12,48]{2,0,1:T(2,128)(2,1)} %param.5), channel_id=1, source_target_pairs={{0,14},{2,0},{4,2},{6,4},{8,6},{10,8},{12,10},{14,12},{1,15},{3,1}... | collective-permute-start | bytes 6920 | tf_op jit(solution)/shard_map/ppermute | solution.py:15
  12.5 1.8 %collective-permute-done = bf16[2,12,48]{2,0,1:T(2,128)(2,1)S(1)} collective-permute-done((bf16[2,12,48]{2,0,1:T(2,128)(2,1)}, bf16[2,12,48]{2,0,1:T(2,128)(2,1)S(1)}, u32[]{:S(2)}, u32[]{:S(2)}) %collective-permute-start) | collective-permute-done | bytes 2336 | tf_op jit(solution)/shard_map/ppermute | solution.py:13
  14.3 0.0 collective-permute-start.1
  14.3 0.0 collective-permute-done.4
  14.3 4.7 %collective-permute-start.5 = (bf16[2,12,48]{2,0,1:T(2,128)(2,1)S(1)}, bf16[2,12,48]{2,0,1:T(2,128)(2,1)S(1)}, u32[]{:S(2)}, u32[]{:S(2)}) collective-permute-start(bf16[2,12,48]{2,0,1:T(2,128)(2,1)S(1)} %collective-permute-done.4), channel_id=1, source_target_pairs={{0,14},{2,0},{4,2},{6,4},{8,6},{10,8},{12,10},{14,12},{1,15},{3,1}... | collective-permute-start | bytes 6920 | tf_op jit(solution)/shard_map/ppermute | solution.py:15
  19.1 1.6 %collective-permute-done.1 = bf16[2,12,48]{2,0,1:T(2,128)(2,1)S(1)} collective-permute-done((bf16[2,12,48]{2,0,1:T(2,128)(2,1)S(1)}, bf16[2,12,48]{2,0,1:T(2,128)(2,1)S(1)}, u32[]{:S(2)}, u32[]{:S(2)}) %collective-permute-start.1) | collective-permute-done | bytes 2336 | tf_op jit(solution)/shard_map/ppermute | solution.py:13
  20.7 4.7 %collective-permute-start.6 = (bf16[2,12,48]{2,0,1:T(2,128)(2,1)S(1)}, bf16[2,12,48]{2,0,1:T(2,128)(2,1)S(1)}, u32[]{:S(2)}, u32[]{:S(2)}) collective-permute-start(bf16[2,12,48]{2,0,1:T(2,128)(2,1)S(1)} %collective-permute-done.5), channel_id=1, source_target_pairs={{0,14},{2,0},{4,2},{6,4},{8,6},{10,8},{12,10},{14,12},{1,15},{3,1}... | collective-permute-start | bytes 6920 | tf_op jit(solution)/shard_map/ppermute | solution.py:15
  25.4 1.6 %collective-permute-done.2 = bf16[2,12,48]{2,0,1:T(2,128)(2,1)S(1)} collective-permute-done((bf16[2,12,48]{2,0,1:T(2,128)(2,1)S(1)}, bf16[2,12,48]{2,0,1:T(2,128)(2,1)S(1)}, u32[]{:S(2)}, u32[]{:S(2)}) %collective-permute-start.2) | collective-permute-done | bytes 2336 | tf_op jit(solution)/shard_map/ppermute | solution.py:13
  27.0 0.0 collective-permute-start.3
  27.0 0.8 slice_bitcast_fusion
  27.8 1.7 %reshape.14 = bf16[17,48,512]{2,1,0:T(8,128)(2,1)S(1)} reshape(bf16[17,48,4,128]{3,2,1,0:T(4,128)(2,1)} %param.3) | data formatting | bytes 1671168 | tf_op jit(solution)/shard_map/reshape | solution.py:21
  29.5 3.8 %collective-permute-done.3 = bf16[2,12,48]{2,0,1:T(2,128)(2,1)S(1)} collective-permute-done((bf16[2,12,48]{2,0,1:T(2,128)(2,1)S(1)}, bf16[2,12,48]{2,0,1:T(2,128)(2,1)S(1)}, u32[]{:S(2)}, u32[]{:S(2)}) %collective-permute-start.3) | collective-permute-done | bytes 2336 | tf_op jit(solution)/shard_map/ppermute | solution.py:13
  33.3 0.2 concatenate.6
  33.6 0.1 reshape.12
  33.7 0.2 convolution_convert_fusion
  33.9 0.1 reshape.13
  34.0 0.2 fusion.2
  34.3 0.1 broadcast_in_dim.2
  34.3 2.1 %scatter_fusion = f32[16,12,512]{2,1,0:T(8,128)S(1)} fusion(f32[16,12,512]{2,1,0:T(8,128)S(1)} %broadcast_in_dim.2, s32[17]{0:T(128)S(1)} %get-tuple-element.6, f32[17,12,512]{2,1,0:T(8,128)S(1)} %fusion.2), kind=kCustom, calls=%fused_computation | custom fusion | flops 104448 | bytes 1253444 | tf_op jit(solution)/shard_map/scatter-add | solution.py:37
  36.5 0.8 copy-done
  37.2 0.0 reduce-scatter.2.cloned.1.call-update
  37.3 59.9 %reduce-scatter.2.cloned.1.call-done = f32[2,12,512]{2,1,0:T(8,128)} async-done(((f32[16,12,512]{2,1,0:T(8,128)}), f32[2,12,512]{2,1,0:T(8,128)}) %reduce-scatter.2.cloned.1.call-update) | async-done | bytes 49168 | tf_op jit(solution)/shard_map/reduce_scatter | solution.py:39
  97.2 1.5 %reshape.24 = f32[2,12,4,128]{3,2,1,0:T(4,128)} reshape(f32[2,12,512]{2,1,0:T(8,128)} %reduce-scatter.2.cloned.1.call-done) | data formatting | bytes 98304 | tf_op jit(solution)/shard_map/reshape | solution.py:40
  (9 shorter events, 0.1 us)
Async XLA Ops:
  6.5 90.6 %reduce-scatter.2.cloned.1.call-start = ((), (), s32[]{:S(2)}) async-start(), calls=%async_computation.1 | async-start | bytes 589824 | tf_op jit(solution)/shard_map/reduce_scatter | solution.py:39
  6.5 7.8 %collective-permute-start = (bf16[2,12,48]{2,0,1:T(2,128)(2,1)}, bf16[2,12,48]{2,0,1:T(2,128)(2,1)S(1)}, u32[]{:S(2)}, u32[]{:S(2)}) collective-permute-start(bf16[2,12,48]{2,0,1:T(2,128)(2,1)} %param.5), channel_id=1, source_target_pairs={{0,2},{2,4},{4,6},{6,8},{8,10},{10,12},{12,14},{14,0},{1,3},{3,5},... | collective-permute-start | bytes 6920 | tf_op jit(solution)/shard_map/ppermute | solution.py:13
  9.5 4.9 %collective-permute-start.4 = (bf16[2,12,48]{2,0,1:T(2,128)(2,1)}, bf16[2,12,48]{2,0,1:T(2,128)(2,1)S(1)}, u32[]{:S(2)}, u32[]{:S(2)}) collective-permute-start(bf16[2,12,48]{2,0,1:T(2,128)(2,1)} %param.5), channel_id=1, source_target_pairs={{0,14},{2,0},{4,2},{6,4},{8,6},{10,8},{12,10},{14,12},{1,15},{3,1}... | collective-permute-start | bytes 6920 | tf_op jit(solution)/shard_map/ppermute | solution.py:15
  14.3 6.3 %collective-permute-start.1 = (bf16[2,12,48]{2,0,1:T(2,128)(2,1)S(1)}, bf16[2,12,48]{2,0,1:T(2,128)(2,1)S(1)}, u32[]{:S(2)}, u32[]{:S(2)}) collective-permute-start(bf16[2,12,48]{2,0,1:T(2,128)(2,1)S(1)} %collective-permute-done), channel_id=1, source_target_pairs={{0,2},{2,4},{4,6},{6,8},{8,10},{10,12},{12,14},{14,0},{1,3},{3,5},... | collective-permute-start | bytes 6920 | tf_op jit(solution)/shard_map/ppermute | solution.py:13
  14.3 6.3 %collective-permute-start.5 = (bf16[2,12,48]{2,0,1:T(2,128)(2,1)S(1)}, bf16[2,12,48]{2,0,1:T(2,128)(2,1)S(1)}, u32[]{:S(2)}, u32[]{:S(2)}) collective-permute-start(bf16[2,12,48]{2,0,1:T(2,128)(2,1)S(1)} %collective-permute-done.4), channel_id=1, source_target_pairs={{0,14},{2,0},{4,2},{6,4},{8,6},{10,8},{12,10},{14,12},{1,15},{3,1}... | collective-permute-start | bytes 6920 | tf_op jit(solution)/shard_map/ppermute | solution.py:15
  20.7 6.3 %collective-permute-start.2 = (bf16[2,12,48]{2,0,1:T(2,128)(2,1)S(1)}, bf16[2,12,48]{2,0,1:T(2,128)(2,1)S(1)}, u32[]{:S(2)}, u32[]{:S(2)}) collective-permute-start(bf16[2,12,48]{2,0,1:T(2,128)(2,1)S(1)} %collective-permute-done.1), channel_id=1, source_target_pairs={{0,2},{2,4},{4,6},{6,8},{8,10},{10,12},{12,14},{14,0},{1,3},{3,5},... | collective-permute-start | bytes 6920 | tf_op jit(solution)/shard_map/ppermute | solution.py:13
  20.7 8.8 %collective-permute-start.6 = (bf16[2,12,48]{2,0,1:T(2,128)(2,1)S(1)}, bf16[2,12,48]{2,0,1:T(2,128)(2,1)S(1)}, u32[]{:S(2)}, u32[]{:S(2)}) collective-permute-start(bf16[2,12,48]{2,0,1:T(2,128)(2,1)S(1)} %collective-permute-done.5), channel_id=1, source_target_pairs={{0,14},{2,0},{4,2},{6,4},{8,6},{10,8},{12,10},{14,12},{1,15},{3,1}... | collective-permute-start | bytes 6920 | tf_op jit(solution)/shard_map/ppermute | solution.py:15
  27.0 6.3 %collective-permute-start.3 = (bf16[2,12,48]{2,0,1:T(2,128)(2,1)S(1)}, bf16[2,12,48]{2,0,1:T(2,128)(2,1)S(1)}, u32[]{:S(2)}, u32[]{:S(2)}) collective-permute-start(bf16[2,12,48]{2,0,1:T(2,128)(2,1)S(1)} %collective-permute-done.2), channel_id=1, source_target_pairs={{0,2},{2,4},{4,6},{6,8},{8,10},{10,12},{12,14},{14,0},{1,3},{3,5},... | collective-permute-start | bytes 6920 | tf_op jit(solution)/shard_map/ppermute | solution.py:13
  27.7 5.6 %copy-start.1 = (bf16[2,12,48]{2,0,1:T(2,128)(2,1)S(1)}, bf16[2,12,48]{2,0,1:T(2,128)(2,1)}, u32[]{:S(2)}) copy-start(bf16[2,12,48]{2,0,1:T(2,128)(2,1)} %param.5) | copy-start | bytes 6916
  36.4 0.8 copy-start
Sparse Core Ops, SparseCore 0:
  37.4 59.7 reduce-scatter.1
